TPU v7x, 768 devices: a whole 4x8x12 slice. The times are simulated.
768 devices in a mesh: blk: 128 (over z_hi, y, x, core), grp: 6 (over z_lo).
Axes of the slice: x: 4, y: 8, z: 12 (z_hi: 2, z_lo: 6; z = z_hi * 6 + z_lo), core: 2. Of those that a mesh axis runs over, the one named last changes fastest.
Arguments:
- images: bfloat16 [24576, 1152], P('blk'), may hold values from -0.1875 to 0.1875
- captions: bfloat16 [221184, 1152], P(('blk', 'grp')), may hold values from -0.1875 to 0.1875
- counts: int32 [24576], P('blk'), may hold values from 1 to 8, as said below
- owners: int32 [221184], P(('blk', 'grp')), may hold values from 0 to 192, as said below
- labels: int32 [221184], P(('blk', 'grp')), may hold values 0 or 1
- logit_scale: float32 [1], replicated, may hold values from 4 to 12
- logit_bias: float32 [1], replicated, may hold values from -4 to -1
Outputs:
- caption_grad: bfloat16 [221184, 1152], P(('blk', 'grp'))
- image_grad: bfloat16 [24576, 1152], P('blk')
Inputs may be any that keep to these rules, and one draw needn't show every extreme that they name: `counts`: within each block of 192 images every count from 1 to 8 occurs equally often. `owners`: on each device the live slots come first and the rest hold 192. Taken device by device along grp, the live slots of a group list the block's images in order, image i repeated counts[i] times. A device holds at most 288 live slots, and in every group one device holds exactly 288.
All inputs are finite; a program needn't handle non-finite values. No bound on the sum of `labels` on one device may be relied on, other than what follows from the above.
Results may differ from a plain program's by a relative error of at most 0.014.
Values may be sent and summed in bfloat16 or wider, within the bound.
A program may use at most 32 MiB of HBM per device.

v0:
```python
import jax
import jax.numpy as jnp
from jax import lax
from jax.sharding import PartitionSpec as P

STEPS = 4


EPSILON = 1e-06


def from_behind(array, axis, by):
    peers = lax.axis_size(axis)
    return lax.ppermute(array, axis, [(i, (i + by) % peers) for i in range(peers)])


def normalize(matrix):
    values = matrix.astype(jnp.float32)
    inverse_norm = lax.rsqrt(jnp.sum(values * values, axis=-1, keepdims=True) + EPSILON)
    return (values * inverse_norm, inverse_norm)


def tangent(unit_float, inverse_norm, direction):
    return inverse_norm * (
        direction - unit_float * jnp.sum(unit_float * direction, axis=-1, keepdims=True)
    )


def pair_terms(caption_unit, weight_float, image_block, logit_gain, logit_shift):
    scores = lax.dot_general(
        caption_unit, image_block, (((1,), (1,)), ((), ())), preferred_element_type=jnp.float32
    )
    pair_coef = (
        logit_gain * weight_float[:, None] * jax.nn.sigmoid(logit_gain * scores + logit_shift)
    ).astype(jnp.bfloat16)
    along_sum = jnp.dot(pair_coef, image_block, preferred_element_type=jnp.float32)
    image_part = lax.dot_general(
        pair_coef, caption_unit, (((0,), (0,)), ((), ())), preferred_element_type=jnp.float32
    )
    return (along_sum, image_part)


def window_terms(caption_unit, weight_float, image_unit, logit_gain, logit_shift):
    along_total = jnp.zeros(caption_unit.shape, jnp.float32)
    partials = []
    image_block = image_unit
    for window_step in range(STEPS + 1):
        if window_step > 0:
            image_block = from_behind(image_block, "blk", 1)
        along_sum, image_part = pair_terms(
            caption_unit, weight_float, image_block, logit_gain, logit_shift
        )
        along_total = along_total + along_sum
        partials.append(image_part)
    return (along_total, partials)


def on_device(images, captions, counts, owners, labels, logit_scale, logit_bias):
    logit_gain = logit_scale[0]
    logit_shift = logit_bias[0]
    image_rows = images.shape[0]
    image_float, image_rate = normalize(images)
    image_unit = image_float.astype(jnp.bfloat16)
    caption_float, caption_rate = normalize(captions)
    caption_unit = caption_float.astype(jnp.bfloat16)
    matches = owners[:, None] == jnp.arange(image_rows, dtype=jnp.int32)[None, :]
    owned_count = jnp.sum(jnp.where(matches, counts[None, :], 0), axis=1)
    live_slot = owners < image_rows
    weight = jnp.where(
        live_slot, 1.0 / jnp.maximum(owned_count, 1).astype(jnp.float32), 0.0
    ).astype(jnp.bfloat16)
    signed = (weight.astype(jnp.float32) * labels.astype(jnp.float32)).astype(jnp.bfloat16)
    along_local, partials = window_terms(
        caption_unit, weight.astype(jnp.float32), image_unit, logit_gain, logit_shift
    )
    along_rounded = along_local.astype(jnp.bfloat16)
    chosen = jnp.where(matches, signed[:, None], jnp.zeros((), jnp.bfloat16))
    correction = lax.dot_general(
        chosen, caption_unit, (((0,), (0,)), ((), ())), preferred_element_type=jnp.float32
    )
    partials[0] = partials[0] - logit_gain * correction
    returned = partials[STEPS]
    for window_step in range(STEPS - 1, -1, -1):
        returned = from_behind(returned, "blk", -1) + partials[window_step]
    image_total = lax.psum(returned, "grp")
    image_grad = tangent(image_float, image_rate, image_total).astype(jnp.bfloat16)
    along_float = lax.optimization_barrier(along_rounded).astype(jnp.float32)
    own_image = jnp.dot(
        matches.astype(jnp.bfloat16), image_unit, preferred_element_type=jnp.float32
    )
    direction = along_float - logit_gain * signed.astype(jnp.float32)[:, None] * own_image
    caption_grad = tangent(caption_float, caption_rate, direction).astype(jnp.bfloat16)
    return (caption_grad, image_grad)


def solution(mesh):
    return jax.shard_map(
        on_device,
        mesh=mesh,
        in_specs=(
            P("blk", None),
            P(("blk", "grp"), None),
            P("blk"),
            P(("blk", "grp")),
            P(("blk", "grp")),
            P(),
            P(),
        ),
        out_specs=(P(("blk", "grp"), None), P("blk", None)),
        check_vma=False,
    )
```

profile of v0, /device:TPU:1, one launch (start us, length us, event | category | flops | bytes accessed | tf_op | source)
XLA Modules:
  0.0 344.4 jit_solution(8755622539557553754)
XLA Ops:
  7.2 0.0 all-reduce.2.cloned.1.call-start
  7.2 1.2 fusion.51
  8.5 1.2 fusion.46
  9.7 4.5 %collective-permute-start = (bf16[192,1152]{1,0:T(8,128)(2,1)S(1)}, bf16[192,1152]{1,0:T(8,128)(2,1)S(1)}, u32[]{:S(2)}, u32[]{:S(2)}) collective-permute-start(bf16[192,1152]{1,0:T(8,128)(2,1)S(1)} %fusion.46), channel_id=1, source_target_pairs={{0,6},{6,12},{12,18},{18,24},{24,30},{30,36},{36,42},{42,48},{48,5... | collective-permute-start | bytes 1327112 | tf_op jit(solution)/shard_map/ppermute | solution.py:14
  14.2 9.2 %collective-permute-done = bf16[192,1152]{1,0:T(8,128)(2,1)S(1)} collective-permute-done((bf16[192,1152]{1,0:T(8,128)(2,1)S(1)}, bf16[192,1152]{1,0:T(8,128)(2,1)S(1)}, u32[]{:S(2)}, u32[]{:S(2)}) %collective-permute-start) | collective-permute-done | bytes 442400 | tf_op jit(solution)/shard_map/ppermute | solution.py:14
  23.4 1.9 collective-permute-start.1
  25.3 22.8 %collective-permute-done.1 = bf16[192,1152]{1,0:T(8,128)(2,1)S(1)} collective-permute-done((bf16[192,1152]{1,0:T(8,128)(2,1)S(1)}, bf16[192,1152]{1,0:T(8,128)(2,1)S(1)}, u32[]{:S(2)}, u32[]{:S(2)}) %collective-permute-start.1) | collective-permute-done | bytes 442400 | tf_op jit(solution)/shard_map/ppermute | solution.py:14
  48.0 1.9 collective-permute-start.2
  51.3 26.4 %collective-permute-done.2 = bf16[192,1152]{1,0:T(8,128)(2,1)S(1)} collective-permute-done((bf16[192,1152]{1,0:T(8,128)(2,1)S(1)}, bf16[192,1152]{1,0:T(8,128)(2,1)S(1)}, u32[]{:S(2)}, u32[]{:S(2)}) %collective-permute-start.2) | collective-permute-done | bytes 442400 | tf_op jit(solution)/shard_map/ppermute | solution.py:14
  77.7 1.9 collective-permute-start.3
  79.6 0.0 copy-done.5
  79.6 0.2 select_reduce_fusion
  79.8 0.2 fusion.8
  80.1 22.5 %collective-permute-done.3 = bf16[192,1152]{1,0:T(8,128)(2,1)S(1)} collective-permute-done((bf16[192,1152]{1,0:T(8,128)(2,1)S(1)}, bf16[192,1152]{1,0:T(8,128)(2,1)S(1)}, u32[]{:S(2)}, u32[]{:S(2)}) %collective-permute-start.3) | collective-permute-done | bytes 442400 | tf_op jit(solution)/shard_map/ppermute | solution.py:14
  102.5 0.5 fusion.43
  103.0 0.0 copy-start.4
  103.0 0.5 fusion.68
  103.5 18.9 %collective-permute-start.4 = (f32[192,1152]{1,0:T(8,128)S(1)}, f32[192,1152]{1,0:T(8,128)S(1)}, u32[]{:S(2)}, u32[]{:S(2)}) collective-permute-start(f32[192,1152]{1,0:T(8,128)S(1)} %fusion.68), channel_id=1, source_target_pairs={{0,762},{6,0},{12,6},{18,12},{24,18},{30,24},{36,30},{42,36},{48,4... | collective-permute-start | bytes 2654216 | tf_op jit(solution)/shard_map/ppermute | solution.py:14
  122.5 0.6 convolution_multiply_fusion.1
  123.1 0.5 fusion.42
  123.6 0.9 collective-permute-done.4
  124.5 0.5 convolution_add_fusion.4
  125.0 17.3 %collective-permute-start.5 = (f32[192,1152]{1,0:T(8,128)S(1)}, f32[192,1152]{1,0:T(8,128)S(1)}, u32[]{:S(2)}, u32[]{:S(2)}) collective-permute-start(f32[192,1152]{1,0:T(8,128)S(1)} %convolution_add_fusion.4), channel_id=1, source_target_pairs={{0,762},{6,0},{12,6},{18,12},{24,18},{30,24},{36,30},{42,36},{48,4... | collective-permute-start | bytes 2654216 | tf_op jit(solution)/shard_map/ppermute | solution.py:14
  142.3 0.5 fusion.39
  142.8 0.5 convolution_subtract_fusion
  143.3 0.5 fusion.41
  143.8 0.5 fusion.65
  144.3 0.0 collective-permute-done.5
  144.4 0.1 add.105
  144.5 29.8 %collective-permute-start.6 = (f32[192,1152]{1,0:T(8,128)S(1)}, f32[192,1152]{1,0:T(8,128)S(1)}, u32[]{:S(2)}, u32[]{:S(2)}) collective-permute-start(f32[192,1152]{1,0:T(8,128)S(1)} %add.105), channel_id=1, source_target_pairs={{0,762},{6,0},{12,6},{18,12},{24,18},{30,24},{36,30},{42,36},{48,4... | collective-permute-start | bytes 2654216 | tf_op jit(solution)/shard_map/ppermute | solution.py:14
  174.3 0.3 fusion.77
  174.6 0.5 fusion.40
  175.1 0.5 fusion.63
  175.6 0.3 convolution_add_fusion.3
  176.0 0.3 collective-permute-done.6
  176.3 0.1 add.106
  176.4 29.6 %collective-permute-start.7 = (f32[192,1152]{1,0:T(8,128)S(1)}, f32[192,1152]{1,0:T(8,128)S(1)}, u32[]{:S(2)}, u32[]{:S(2)}) collective-permute-start(f32[192,1152]{1,0:T(8,128)S(1)} %add.106), channel_id=1, source_target_pairs={{0,762},{6,0},{12,6},{18,12},{24,18},{30,24},{36,30},{42,36},{48,4... | collective-permute-start | bytes 2654216 | tf_op jit(solution)/shard_map/ppermute | solution.py:14
  206.0 0.3 convolution_add_fusion.2
  206.3 0.3 convolution_add_fusion.1
  206.7 0.3 fusion
  207.0 1.0 collective-permute-done.7
  208.0 1.1 add.107
  209.1 0.0 all-reduce.2.cloned.1.call-update
  209.1 0.6 fusion.4
  209.7 1.2 fusion.7
  211.0 124.0 %all-reduce.2.cloned.1.call-done = f32[192,1152]{1,0:T(8,128)} async-done(((f32[192,1152]{1,0:T(8,128)}), f32[192,1152]{1,0:T(8,128)}) %all-reduce.2.cloned.1.call-update) | async-done | bytes 884752 | tf_op jit(solution)/shard_map/psum | solution.py:85
  335.0 1.5 fusion.47
  336.5 1.0 fusion.50
  (13 shorter events, 0.0 us)
Async XLA Ops:
  7.2 72.4 %copy-start.5 = (s32[192]{0:T(256)S(1)}, s32[192]{0:T(256)}, u32[]{:S(2)}) copy-start(s32[192]{0:T(256)} %param.9) | copy-start | bytes 2308
  7.2 72.4 %copy-start.3 = (s32[288]{0:T(512)S(1)}, s32[288]{0:T(512)}, u32[]{:S(2)}) copy-start(s32[288]{0:T(512)} %param.10) | copy-start | bytes 3460
  7.2 72.6 %copy-start = (bf16[288,1152]{1,0:T(8,128)(2,1)S(1)}, bf16[288,1152]{1,0:T(8,128)(2,1)}, u32[]{:S(2)}) copy-start(bf16[288,1152]{1,0:T(8,128)(2,1)} %param.8) | copy-start | bytes 1990660
  7.2 327.8 %all-reduce.2.cloned.1.call-start = ((), (), s32[]{:S(2)}) async-start(), calls=%async_computation | async-start | bytes 1769472 | tf_op jit(solution)/shard_map/psum | solution.py:85
  9.7 13.7 %collective-permute-start = (bf16[192,1152]{1,0:T(8,128)(2,1)S(1)}, bf16[192,1152]{1,0:T(8,128)(2,1)S(1)}, u32[]{:S(2)}, u32[]{:S(2)}) collective-permute-start(bf16[192,1152]{1,0:T(8,128)(2,1)S(1)} %fusion.46), channel_id=1, source_target_pairs={{0,6},{6,12},{12,18},{18,24},{24,30},{30,36},{36,42},{42,48},{48,5... | collective-permute-start | bytes 1327112 | tf_op jit(solution)/shard_map/ppermute | solution.py:14
  23.4 24.7 %collective-permute-start.1 = (bf16[192,1152]{1,0:T(8,128)(2,1)S(1)}, bf16[192,1152]{1,0:T(8,128)(2,1)S(1)}, u32[]{:S(2)}, u32[]{:S(2)}) collective-permute-start(bf16[192,1152]{1,0:T(8,128)(2,1)S(1)} %collective-permute-done), channel_id=1, source_target_pairs={{0,6},{6,12},{12,18},{18,24},{24,30},{30,36},{36,42},{42,48},{48,5... | collective-permute-start | bytes 1327112 | tf_op jit(solution)/shard_map/ppermute | solution.py:14
  48.0 29.6 %collective-permute-start.2 = (bf16[192,1152]{1,0:T(8,128)(2,1)S(1)}, bf16[192,1152]{1,0:T(8,128)(2,1)S(1)}, u32[]{:S(2)}, u32[]{:S(2)}) collective-permute-start(bf16[192,1152]{1,0:T(8,128)(2,1)S(1)} %collective-permute-done.1), channel_id=1, source_target_pairs={{0,6},{6,12},{12,18},{18,24},{24,30},{30,36},{36,42},{42,48},{48,5... | collective-permute-start | bytes 1327112 | tf_op jit(solution)/shard_map/ppermute | solution.py:14
  77.7 24.9 %collective-permute-start.3 = (bf16[192,1152]{1,0:T(8,128)(2,1)S(1)}, bf16[192,1152]{1,0:T(8,128)(2,1)S(1)}, u32[]{:S(2)}, u32[]{:S(2)}) collective-permute-start(bf16[192,1152]{1,0:T(8,128)(2,1)S(1)} %collective-permute-done.2), channel_id=1, source_target_pairs={{0,6},{6,12},{12,18},{18,24},{24,30},{30,36},{36,42},{42,48},{48,5... | collective-permute-start | bytes 1327112 | tf_op jit(solution)/shard_map/ppermute | solution.py:14
  103.0 19.5 %copy-start.4 = (s32[288]{0:T(512)S(1)}, s32[288]{0:T(512)}, u32[]{:S(2)}) copy-start(s32[288]{0:T(512)} %param.11) | copy-start | bytes 3460
  103.5 20.9 %collective-permute-start.4 = (f32[192,1152]{1,0:T(8,128)S(1)}, f32[192,1152]{1,0:T(8,128)S(1)}, u32[]{:S(2)}, u32[]{:S(2)}) collective-permute-start(f32[192,1152]{1,0:T(8,128)S(1)} %fusion.68), channel_id=1, source_target_pairs={{0,762},{6,0},{12,6},{18,12},{24,18},{30,24},{36,30},{42,36},{48,4... | collective-permute-start | bytes 2654216 | tf_op jit(solution)/shard_map/ppermute | solution.py:14
  125.0 19.3 %collective-permute-start.5 = (f32[192,1152]{1,0:T(8,128)S(1)}, f32[192,1152]{1,0:T(8,128)S(1)}, u32[]{:S(2)}, u32[]{:S(2)}) collective-permute-start(f32[192,1152]{1,0:T(8,128)S(1)} %convolution_add_fusion.4), channel_id=1, source_target_pairs={{0,762},{6,0},{12,6},{18,12},{24,18},{30,24},{36,30},{42,36},{48,4... | collective-permute-start | bytes 2654216 | tf_op jit(solution)/shard_map/ppermute | solution.py:14
  144.5 31.9 %collective-permute-start.6 = (f32[192,1152]{1,0:T(8,128)S(1)}, f32[192,1152]{1,0:T(8,128)S(1)}, u32[]{:S(2)}, u32[]{:S(2)}) collective-permute-start(f32[192,1152]{1,0:T(8,128)S(1)} %add.105), channel_id=1, source_target_pairs={{0,762},{6,0},{12,6},{18,12},{24,18},{30,24},{36,30},{42,36},{48,4... | collective-permute-start | bytes 2654216 | tf_op jit(solution)/shard_map/ppermute | solution.py:14
  176.4 31.6 %collective-permute-start.7 = (f32[192,1152]{1,0:T(8,128)S(1)}, f32[192,1152]{1,0:T(8,128)S(1)}, u32[]{:S(2)}, u32[]{:S(2)}) collective-permute-start(f32[192,1152]{1,0:T(8,128)S(1)} %add.106), channel_id=1, source_target_pairs={{0,762},{6,0},{12,6},{18,12},{24,18},{30,24},{36,30},{42,36},{48,4... | collective-permute-start | bytes 2654216 | tf_op jit(solution)/shard_map/ppermute | solution.py:14
  209.7 125.3 %copy-start.1 = (bf16[192,1152]{1,0:T(8,128)(2,1)S(1)}, bf16[192,1152]{1,0:T(8,128)(2,1)}, u32[]{:S(2)}) copy-start(bf16[192,1152]{1,0:T(8,128)(2,1)} %param.7) | copy-start | bytes 1327108
  335.0 1.5 copy-start.2
Sparse Core Ops, SparseCore 0:
  209.2 125.7 all-reduce.1
where the time goes:
time: 348 us; the launch traced here: 344 us
  waiting for transfers between devices  207 us (59%)
  starting transfers between devices  106 us (30%)
  between operations  15.6 us (4%)
  matrix products  7.9 us (2%)
  other arithmetic  7.86 us (2%)
    psum x1, waiting for transfers between devices, on_device(): image_total = lax.psum(returned, 'grp')  124 us
    ppermute x8, starting transfers between devices, from_behind(): lax.ppermute(array, axis, [(i, (i + by) % peers) for i in range(peers)])  106 us
    ppermute x8, waiting for transfers between devices, from_behind(): lax.ppermute(array, axis, [(i, (i + by) % peers) for i in range(peers)])  83.1 us
  transfers between devices with their start and end apart: 9, of which 8 were waited for; matrix products, arithmetic and copies ran while one was open for 2% of the time, Pallas kernels for 0%

commit v1 on v0

v1 whole, which is shorter than its diff:
```python
import functools

import jax
import jax.numpy as jnp
from jax import lax
from jax.experimental import pallas as pl
from jax.experimental.pallas import tpu as pltpu
from jax.sharding import PartitionSpec as P

MESH = pl.DeviceIdType.MESH
EPSILON = 1e-06
BLKS = 128
HALF = 32
IMG = 192
CAP = 288
D = 1152
ROWS = 48
CHUNKS = IMG // ROWS
SHARD = ROWS // 3
STEPS = 4
LAG_D = 2
LAG_Y = 3
LAG_E = 4

NEAR, FAR, SIB1, SIB3, Q1, Q3, NEARB, FARB, EDGEN, EDGEF, RS1, RS2, EX, AG1, AG2, SWAP, SWAPB = range(17)
FANN, FANF = 17, 20
FARX, FARM1, FARM2 = 23, 24, 25
KINDS = 26

F32 = jnp.float32
BF16 = jnp.bfloat16


def column(row, n):
    eye = lax.broadcasted_iota(jnp.int32, (n, n), 0) == lax.broadcasted_iota(jnp.int32, (n, n), 1)
    return jnp.sum(jnp.where(eye, row, 0.0), axis=1, keepdims=True)


def kernel(
    img_hbm, cap_hbm, cnt_hbm, own_hbm, lab_hbm, gain_ref, shift_ref,
    cg_ref, ig_ref,
    unit, imgf, rate, capu, capr, wcol, corr, ownd, along, part, own32,
    g_buf, p_buf, q_buf, sn, sf, rn, rf, swap, edgen, edgef, back, swapb, t16, rs, x16, xr, grad,
    img_ref, cap_ref, cnt_ref, own_ref, lab_ref, lsem, ssem, rsem,
):
    blk = lax.axis_index("blk")
    g = lax.axis_index("grp")
    c = lax.rem(blk, 2)
    mm = lax.rem(blk // 2, HALF)
    tri = g // 3
    p = lax.rem(g, 3)
    gain = gain_ref[0]
    shift = shift_ref[0]
    fc = c.astype(F32)

    n_out_x, f_out_x = mm == HALF - 1, mm >= HALF - 2
    n_in_x, f_in_x = mm == 0, mm <= 1
    second = mm == 1
    n_reg_next, f_reg_next = jnp.logical_not(n_out_x), jnp.logical_not(f_out_x)
    n_reg_prev, f_reg_prev = jnp.logical_not(n_in_x), jnp.logical_not(f_in_x)
    n_next = (lax.rem(blk + 2, BLKS), g)
    f_next = (lax.rem(blk + 4, BLKS), g)
    n_prev = (lax.rem(blk + BLKS - 2, BLKS), g)
    f_prev = (lax.rem(blk + BLKS - 4, BLKS), g)
    sib = (blk + 1 - 2 * c, g)
    base = blk - 2 * mm

    def plane(s):
        return 3 * tri + s

    mates = [(blk, plane(lax.rem(p + d, 3))) for d in (1, 2)]
    across = (blk, 3 * (1 - tri) + p)
    twin = (lax.rem(blk + 2 * HALF, BLKS), 3 * (1 - tri) + p)
    fan_n = [(base, plane(s)) for s in range(3)]
    fan_f = (jnp.where(n_out_x, base + 2, base), g)
    fan_f_all = [(fan_f[0], plane(s)) for s in range(3)]
    from_n = [(base + 2 * HALF - 2, plane(s)) for s in range(3)]
    from_f = [(jnp.where(second, base + 2 * HALF - 2, base + 2 * HALF - 4), plane(s)) for s in range(3)]

    def copy(kind, r, src, dst, dev, recv=None):
        return pltpu.make_async_remote_copy(
            src_ref=src,
            dst_ref=dst,
            send_sem=ssem.at[kind, r],
            recv_sem=rsem.at[kind if recv is None else recv, r],
            device_id=dev,
            device_id_type=MESH,
        )

    def slot(r, k):
        return g_buf.at[r, pl.ds(pl.multiple_of(k * ROWS, 16), ROWS)]

    def near(r):
        return copy(NEAR, r, slot(r, 0), slot(r, 2), n_next)

    def far(r):
        return copy(FAR, r, slot(r, 0), slot(r, 4), f_next)

    def third(r, k, s):
        return g_buf.at[r, pl.ds(pl.multiple_of(k * ROWS + s * SHARD, 16), SHARD)]

    def swap_out(r):
        return copy(SWAP, r, third(r, 0, p), swap.at[r], twin)

    def fan_near(r, s):
        return copy(FANN + s, r, swap.at[r], third(r, 2, p), fan_n[s], NEAR)

    def fan_far(r):
        return copy(FARX, r, swap.at[r], third(r, 4, p), fan_f)

    def far_mate(r, d):
        return copy(FARM1 + d - 1, r, third(r, 4, p), third(r, 4, p), mates[d - 1])

    def far_from_mate(r, d):
        s = lax.rem(p + 3 - d, 3)
        return copy(FARM1 + d - 1, r, third(r, 4, s), third(r, 4, s), mates[d - 1])

    def sib1(r):
        return copy(SIB1, r, slot(r, 2 * c), slot(r, 1), sib)

    def sib3(r):
        return copy(SIB3, r, slot(r, 2 + 2 * c), slot(r, 3), sib)

    def q_copy(r, j):
        return copy(Q1 + j, r, p_buf.at[r, j], q_buf.at[r, j], sib)

    def near_back(r):
        return copy(NEARB, r, sn.at[r], rn.at[r], n_prev)

    def far_back(r):
        return copy(FARB, r, sf.at[r], rf.at[r], f_prev)

    def shard(ref, r, s):
        return ref.at[r, pl.ds(pl.multiple_of(s * SHARD, 16), SHARD)]

    def edge_near(r, s):
        return copy(FANN + s, r, shard(sn, r, s), shard(edgen, r, p), from_n[s], EDGEN)

    def edge_far(r, s):
        return copy(FANF + s, r, shard(sf, r, s), shard(edgef, r, p), from_f[s], EDGEF)

    def edge_near_all(r):
        return copy(EDGEN, r, sn.at[r], edgen.at[r], from_n[0])

    def edge_far_all(r):
        return copy(EDGEF, r, sf.at[r], edgef.at[r], from_f[0])

    def swap_back(r):
        return copy(SWAPB, r, back.at[r], swapb.at[r], twin)

    def scatter(r, d):
        s = lax.rem(p + d, 3)
        return copy(RS1 + d - 1, r, shard(t16, r, s), rs.at[r, d - 1], mates[d - 1])

    def exchange(r):
        return copy(EX, r, x16.at[r], xr.at[r], across)

    def gather(r, d):
        return copy(AG1 + d - 1, r, shard(grad, r, p), shard(grad, r, p), mates[d - 1])

    def gathered(r, d):
        s = lax.rem(p + 3 - d, 3)
        return copy(AG1 + d - 1, r, shard(grad, r, s), shard(grad, r, s), mates[d - 1])

    loads = [
        pltpu.make_async_copy(src, dst, lsem.at[k])
        for k, (src, dst) in enumerate(
            (
                (img_hbm, img_ref),
                (cap_hbm, cap_ref),
                (cnt_hbm, cnt_ref),
                (own_hbm, own_ref),
                (lab_hbm, lab_ref),
            )
        )
    ]
    for load in loads:
        load.start()

    barrier = pltpu.get_barrier_semaphore()

    def greet(dev):
        pl.semaphore_signal(barrier, inc=1, device_id=dev, device_id_type=MESH)

    for dev in (sib, mates[0], mates[1], across):
        greet(dev)
    met = jnp.int32(4)
    for has, devs in (
        (n_reg_next, [n_next]),
        (f_reg_next, [f_next]),
        (n_reg_prev, [n_prev]),
        (f_reg_prev, [f_prev]),
        (f_out_x, [twin] + fan_f_all),
        (n_out_x, fan_n),
        (f_in_x, from_f),
        (n_in_x, from_n),
    ):
        for dev in devs:
            pl.when(has)(functools.partial(greet, dev))
        met = met + jnp.where(has, len(devs), 0)

    pl.semaphore_wait(barrier, met)

    loads[0].wait()
    values = img_ref[...].astype(F32)
    image_rate = lax.rsqrt(jnp.sum(values * values, axis=-1, keepdims=True) + EPSILON)
    values = values * image_rate
    rate[...] = image_rate
    imgf[...] = values
    unit[...] = values.astype(BF16)
    for r in range(CHUNKS):
        g_buf[r, 0:ROWS] = unit[r * ROWS : (r + 1) * ROWS]

    for r in range(CHUNKS):
        pl.when(f_out_x)(lambda r=r: swap_out(r).start())
        pl.when(n_reg_next)(lambda r=r: near(r).start())
        pl.when(f_reg_next)(lambda r=r: far(r).start())

    for load in loads[1:]:
        load.wait()
    values = cap_ref[...].astype(F32)
    caption_rate = lax.rsqrt(jnp.sum(values * values, axis=-1, keepdims=True) + EPSILON)
    capr[...] = caption_rate
    capu[...] = (values * caption_rate).astype(BF16)
    owners = column(own_ref[...].reshape(1, CAP).astype(F32), CAP)
    labels = column(lab_ref[...].reshape(1, CAP).astype(F32), CAP)
    matches = owners == lax.broadcasted_iota(jnp.int32, (CAP, IMG), 1).astype(F32)
    owned = jnp.sum(jnp.where(matches, cnt_ref[...].reshape(1, IMG).astype(F32), 0.0), axis=1, keepdims=True)
    weight = jnp.where(owners < float(IMG), 1.0 / jnp.maximum(owned, 1.0), 0.0)
    weight = weight.astype(BF16).astype(F32)
    signed = (weight * labels).astype(BF16).astype(F32)
    wcol[...] = gain * weight
    chosen = jnp.where(matches, signed, 0.0)
    corr[...] = gain * lax.dot_general(
        chosen.T.astype(BF16), capu[...], (((1,), (0,)), ((), ())), preferred_element_type=F32
    )
    picked = jnp.where(matches, 1.0, 0.0).astype(BF16)
    ownd[...] = (gain * signed) * jnp.dot(picked, unit[...], preferred_element_type=F32)
    along[...] = jnp.zeros_like(along)

    def stage_a(r):
        near(r).wait_recv()
        pl.when(f_reg_prev)(lambda: far(r).wait_recv())

        @pl.when(f_in_x)
        def _():
            far_from_mate(r, 1).wait_recv()
            far_from_mate(r, 2).wait_recv()

        sib1(r).start()
        sib3(r).start()
        sib1(r).wait_recv()
        sib3(r).wait_recv()

    def stage_b(r):
        blocks = g_buf[r]
        scores = lax.dot_general(
            capu[...], blocks, (((1,), (1,)), ((), ())), preferred_element_type=F32
        )
        coef = wcol[...] * jax.nn.sigmoid(gain * scores + shift)
        along[...] += jnp.dot(coef.astype(BF16), blocks, preferred_element_type=F32)
        part[...] = jnp.dot(coef.T.astype(BF16), capu[...], preferred_element_type=F32)
        p_buf[r, 0] = part[ROWS : 2 * ROWS].astype(BF16)
        p_buf[r, 1] = part[3 * ROWS : 4 * ROWS].astype(BF16)
        q_copy(r, 0).start()
        q_copy(r, 1).start()
        rows = pl.ds(pl.multiple_of(r * ROWS, 16), ROWS)
        own32[r] = part[0:ROWS] - corr[rows]

    def stage_c(r):
        q_copy(r, 0).wait_recv()
        q_copy(r, 1).wait_recv()
        own32[r] += (1.0 - fc) * q_buf[r, 0].astype(F32)
        sn[r] = (part[2 * ROWS : 3 * ROWS] + q_buf[r, 1 - c].astype(F32)).astype(BF16)
        sf[r] = (part[4 * ROWS : 5 * ROWS] + fc * q_buf[r, 1].astype(F32)).astype(BF16)
        pl.when(n_reg_prev)(lambda: near_back(r).start())
        pl.when(f_reg_prev)(lambda: far_back(r).start())

        @pl.when(n_in_x)
        def _():
            for s in range(3):
                edge_near(r, s).start()

        @pl.when(f_in_x)
        def _():
            for s in range(3):
                edge_far(r, s).start()

    def stage_x(r):
        @pl.when(f_out_x)
        def _():
            swap_out(r).wait_recv()
            fan_far(r).start()

        @pl.when(n_out_x)
        def _():
            for s in range(3):
                fan_near(r, s).start()

    def stage_w(r):
        @pl.when(f_in_x)
        def _():
            fan_far(r).wait_recv()
            far_mate(r, 1).start()
            far_mate(r, 2).start()

    def three(ref, r):
        return (
            ref[r, 0:SHARD].astype(F32)
            + ref[r, SHARD : 2 * SHARD].astype(F32)
            + ref[r, 2 * SHARD : 3 * SHARD].astype(F32)
        )

    def stage_y(r):
        @pl.when(n_out_x)
        def _():
            edge_near_all(r).wait_recv()
            edge_far_all(r).wait_recv()
            back[r] = (three(edgen, r) + three(edgef, r)).astype(BF16)
            swap_back(r).start()

        @pl.when(jnp.logical_and(f_out_x, jnp.logical_not(n_out_x)))
        def _():
            edge_far_all(r).wait_recv()
            back[r] = three(edgef, r).astype(BF16)
            swap_back(r).start()

    def stage_d(r):
        @pl.when(n_reg_next)
        def _():
            near_back(r).wait_recv()
            own32[r] += rn[r].astype(F32)

        @pl.when(f_reg_next)
        def _():
            far_back(r).wait_recv()
            own32[r] += rf[r].astype(F32)

        t16[r] = own32[r].astype(BF16)
        scatter(r, 1).start()
        scatter(r, 2).start()

    def stage_e(r):
        scatter(r, 1).wait_recv()
        scatter(r, 2).wait_recv()
        mine = own32[r, pl.ds(pl.multiple_of(p * SHARD, 16), SHARD)]
        mine = mine + rs[r, 0].astype(F32) + rs[r, 1].astype(F32)
        x16[r] = mine.astype(BF16)

        @pl.when(f_out_x)
        def _():
            swap_back(r).wait_recv()
            x16[r] = (mine + swapb[r].astype(F32)).astype(BF16)

        exchange(r).start()

    def stage_f(r):
        exchange(r).wait_recv()
        total = x16[r].astype(F32) + xr[r].astype(F32)
        rows = pl.ds(pl.multiple_of(r * ROWS + p * SHARD, 16), SHARD)
        v = imgf[rows]
        out = rate[rows] * (total - v * jnp.sum(v * total, axis=-1, keepdims=True))
        grad[r, pl.ds(pl.multiple_of(p * SHARD, 16), SHARD)] = out.astype(BF16)
        gather(r, 1).start()
        gather(r, 2).start()

    def stage_g(r):
        gathered(r, 1).wait_recv()
        gathered(r, 2).wait_recv()
        ig_ref[pl.ds(pl.multiple_of(r * ROWS, 16), ROWS)] = grad[r]

    def caption_out():
        direction = along[...].astype(BF16).astype(F32) - ownd[...]
        u = cap_ref[...].astype(F32) * capr[...]
        turned = direction - u * jnp.sum(u * direction, axis=-1, keepdims=True)
        cg_ref[...] = (capr[...] * turned).astype(BF16)

    for r in range(CHUNKS):
        stage_x(r)
    for r in range(CHUNKS):
        stage_w(r)

    def step(i, carry):
        def at(lag, stage, when=None):
            r = i - lag
            ready = jnp.logical_and(r >= 0, r < CHUNKS)
            if when is not None:
                ready = jnp.logical_and(ready, when)

            @pl.when(ready)
            def _():
                stage(r)

        at(0, stage_a)
        at(0, stage_b)
        at(0, stage_c)
        at(LAG_D, stage_d)
        at(LAG_Y, stage_y, f_out_x)
        for k, stage in enumerate((stage_e, stage_f, stage_g)):
            at(LAG_D + 1 + k, stage, f_reg_next)
            at(LAG_E + k, stage, f_out_x)
        pl.when(i == CHUNKS)(caption_out)
        return carry

    lax.fori_loop(0, CHUNKS + LAG_E + 2, step, 0)

    def sent(r, carry):
        pl.when(n_reg_next)(lambda: near(r).wait_send())
        pl.when(f_reg_next)(lambda: far(r).wait_send())
        sib1(r).wait_send()
        sib3(r).wait_send()
        q_copy(r, 0).wait_send()
        q_copy(r, 1).wait_send()
        pl.when(n_reg_prev)(lambda: near_back(r).wait_send())
        pl.when(f_reg_prev)(lambda: far_back(r).wait_send())

        @pl.when(f_out_x)
        def _():
            swap_out(r).wait_send()
            swap_back(r).wait_send()
            fan_far(r).wait_send()

        @pl.when(n_out_x)
        def _():
            for s in range(3):
                fan_near(r, s).wait_send()

        @pl.when(n_in_x)
        def _():
            for s in range(3):
                edge_near(r, s).wait_send()

        @pl.when(f_in_x)
        def _():
            far_mate(r, 1).wait_send()
            far_mate(r, 2).wait_send()
            for s in range(3):
                edge_far(r, s).wait_send()

        scatter(r, 1).wait_send()
        scatter(r, 2).wait_send()
        exchange(r).wait_send()
        gather(r, 1).wait_send()
        gather(r, 2).wait_send()
        return carry

    lax.fori_loop(0, CHUNKS, sent, 0)


def on_device(images, captions, counts, owners, labels, logit_scale, logit_bias):
    vmem = pl.BlockSpec(memory_space=pltpu.VMEM)
    smem = pl.BlockSpec(memory_space=pltpu.SMEM)
    chunk = (CHUNKS, ROWS, D)
    return pl.pallas_call(
        kernel,
        out_shape=(
            jax.ShapeDtypeStruct((CAP, D), BF16),
            jax.ShapeDtypeStruct((IMG, D), BF16),
        ),
        in_specs=[pl.BlockSpec(memory_space=pltpu.HBM)] * 5 + [smem] * 2,
        out_specs=(vmem, vmem),
        scratch_shapes=[
            pltpu.VMEM((IMG, D), BF16),
            pltpu.VMEM((IMG, D), F32),
            pltpu.VMEM((IMG, 1), F32),
            pltpu.VMEM((CAP, D), BF16),
            pltpu.VMEM((CAP, 1), F32),
            pltpu.VMEM((CAP, 1), F32),
            pltpu.VMEM((IMG, D), F32),
            pltpu.VMEM((CAP, D), F32),
            pltpu.VMEM((CAP, D), F32),
            pltpu.VMEM(((STEPS + 1) * ROWS, D), F32),
            pltpu.VMEM(chunk, F32),
            pltpu.VMEM((CHUNKS, (STEPS + 1) * ROWS, D), BF16),
            pltpu.VMEM((CHUNKS, 2, ROWS, D), BF16),
            pltpu.VMEM((CHUNKS, 2, ROWS, D), BF16),
            pltpu.VMEM(chunk, BF16),
            pltpu.VMEM(chunk, BF16),
            pltpu.VMEM(chunk, BF16),
            pltpu.VMEM(chunk, BF16),
            pltpu.VMEM((CHUNKS, SHARD, D), BF16),
            pltpu.VMEM(chunk, BF16),
            pltpu.VMEM(chunk, BF16),
            pltpu.VMEM((CHUNKS, SHARD, D), BF16),
            pltpu.VMEM((CHUNKS, SHARD, D), BF16),
            pltpu.VMEM(chunk, BF16),
            pltpu.VMEM((CHUNKS, 2, SHARD, D), BF16),
            pltpu.VMEM((CHUNKS, SHARD, D), BF16),
            pltpu.VMEM((CHUNKS, SHARD, D), BF16),
            pltpu.VMEM(chunk, BF16),
            pltpu.VMEM((IMG, D), BF16),
            pltpu.VMEM((CAP, D), BF16),
            pltpu.VMEM((IMG,), jnp.int32),
            pltpu.VMEM((CAP,), jnp.int32),
            pltpu.VMEM((CAP,), jnp.int32),
            pltpu.SemaphoreType.DMA((5,)),
            pltpu.SemaphoreType.DMA((KINDS, CHUNKS)),
            pltpu.SemaphoreType.DMA((KINDS, CHUNKS)),
        ],
        compiler_params=pltpu.CompilerParams(
            collective_id=0, has_side_effects=True, vmem_limit_bytes=55836672
        ),
    )(
        images,
        captions,
        counts,
        owners,
        labels,
        logit_scale,
        logit_bias,
    )


def solution(mesh):
    return jax.shard_map(
        on_device,
        mesh=mesh,
        in_specs=(
            P("blk", None),
            P(("blk", "grp"), None),
            P("blk"),
            P(("blk", "grp")),
            P(("blk", "grp")),
            P(),
            P(),
        ),
        out_specs=(P(("blk", "grp"), None), P("blk", None)),
        check_vma=False,
    )
```

time: 348 us -> 89.7 us (0.26)
  waiting for transfers between devices: 207 us -> 0 us
  starting transfers between devices: 106 us -> 0 us
  Pallas kernels: 0 us -> 82.9 us
  between operations: 15.6 us -> 2 us
  matrix products: 7.9 us -> 0 us
  other arithmetic: 7.86 us -> 0 us
    psum x1 -> x0, waiting for transfers between devices: 124 us -> none  [on_device(): image_total = lax.psum(returned, 'grp')]
    ppermute x8 -> x0, starting transfers between devices: 106 us -> none  [from_behind(): lax.ppermute(array, axis, [(i, (i + by) % peers) for i in range(peers)])]
    ppermute x8 -> x0, waiting for transfers between devices: 83.1 us -> none  [from_behind(): lax.ppermute(array, axis, [(i, (i + by) % peers) for i in range(peers)])]
    pallas_call x0 -> x1, Pallas kernels: none -> 82.9 us  [on_device(): pl.pallas_call(kernel, out_shape=(jax.ShapeDtypeStruct((CAP, D), BF16), j...]
    dot_general x17 -> x0, matrix products: 7.9 us -> none  [the longest x5 2.58 us: pair_terms(): lax.dot_general(pair_coef, caption_unit, (((0,), (0,)), ((), ())), prefer...]
  transfers between devices with their start and end apart: 9 -> 0, of which waited for: 8 -> 0; matrix products, arithmetic and copies ran while one was open for 2% -> 0% of each run, Pallas kernels for 0% -> 0%
where the time goes in v1:
time: 89.7 us; the launch traced here: 88.3 us
  Pallas kernels  82.9 us (92%)
  local copies, waits for them, and re-layouts  3.42 us (4%)
  between operations  2 us (2%)
    pallas_call x1, Pallas kernels, on_device(): pl.pallas_call(kernel, out_shape=(jax.ShapeDtypeStruct((CAP, D), BF16), j...  82.9 us
    unnamed x8, local copies, waits for them, and re-layouts  3.42 us

profile of v1, /device:TPU:1, one launch (start us, length us, event | category | flops | bytes accessed | tf_op | source)
XLA Modules:
  0.0 88.3 jit_solution(3845905163103477541)
XLA Ops:
  0.6 0.0 copy-start
  1.3 0.0 copy-start.2
  2.0 0.0 copy-done
  2.0 0.0 copy-done.2
  2.0 0.0 copy-start.1
  2.0 0.7 copy-done.1
  2.7 82.9 %shard_map.86 = (bf16[288,1152]{1,0:T(8,128)(2,1)}, bf16[192,1152]{1,0:T(8,128)(2,1)S(1)}) custom-call(bf16[192,1152]{1,0:T(8,128)(2,1)} %img_hbm.1, bf16[288,1152]{1,0:T(8,128)(2,1)} %cap_hbm.1, s32[192]{0:T(256)S(1)} %copy-done.2, s32[288]{0:T(512)S(1)} %copy-done, s32[288]{0:T(512)S(1)} %copy-done.1, f32[1]{0:T(128)S(6)} %copy.11.gain_ref, ...), custom_call_target="tpu_custom_call" | custom-call | tf_op jit(solution)/shard_map/pallas_call | solution.py:454
  85.6 2.0 %copy.13 = bf16[288,1152]{1,0:T(8,128)(2,1)} copy(bf16[288,1152]{1,0:T(8,128)(2,1)} %get-tuple-element.4) | data formatting | bytes 1327104
  87.5 0.8 copy.14
Async XLA Ops:
  0.6 1.3 %copy-start = (s32[288]{0:T(512)S(1)}, s32[288]{0:T(512)}, u32[]{:S(2)}) copy-start(s32[288]{0:T(512)} %own_hbm.1) | copy-start | bytes 3460
  1.3 0.7 copy-start.2
  2.0 0.7 copy-start.1

commit v2 on v1

--- a/solution.py
+++ b/solution.py
@@ -19,8 +19,8 @@
 SHARD = ROWS // 3
 STEPS = 4
 LAG_D = 2
-LAG_Y = 3
-LAG_E = 4
+LAG_Y = 4
+LAG_E = 5
 
 NEAR, FAR, SIB1, SIB3, Q1, Q3, NEARB, FARB, EDGEN, EDGEF, RS1, RS2, EX, AG1, AG2, SWAP, SWAPB = range(17)
 FANN, FANF = 17, 20
@@ -199,8 +199,6 @@
             pl.when(has)(functools.partial(greet, dev))
         met = met + jnp.where(has, len(devs), 0)
 
-    pl.semaphore_wait(barrier, met)
-
     loads[0].wait()
     values = img_ref[...].astype(F32)
     image_rate = lax.rsqrt(jnp.sum(values * values, axis=-1, keepdims=True) + EPSILON)
@@ -210,6 +208,8 @@
     unit[...] = values.astype(BF16)
     for r in range(CHUNKS):
         g_buf[r, 0:ROWS] = unit[r * ROWS : (r + 1) * ROWS]
+
+    pl.semaphore_wait(barrier, met)
 
     for r in range(CHUNKS):
         pl.when(f_out_x)(lambda r=r: swap_out(r).start())
@@ -249,10 +249,10 @@
 
         sib1(r).start()
         sib3(r).start()
+
+    def stage_b(r):
         sib1(r).wait_recv()
         sib3(r).wait_recv()
-
-    def stage_b(r):
         blocks = g_buf[r]
         scores = lax.dot_general(
             capu[...], blocks, (((1,), (1,)), ((), ())), preferred_element_type=F32
@@ -377,7 +377,7 @@
 
     for r in range(CHUNKS):
         stage_x(r)
-    for r in range(CHUNKS):
+    for r in range(3):
         stage_w(r)
 
     def step(i, carry):
@@ -392,8 +392,9 @@
                 stage(r)
 
         at(0, stage_a)
+        at(-3, stage_w)
+        at(1, stage_c)
         at(0, stage_b)
-        at(0, stage_c)
         at(LAG_D, stage_d)
         at(LAG_Y, stage_y, f_out_x)
         for k, stage in enumerate((stage_e, stage_f, stage_g)):
@@ -402,7 +403,7 @@
         pl.when(i == CHUNKS)(caption_out)
         return carry
 
-    lax.fori_loop(0, CHUNKS + LAG_E + 2, step, 0)
+    lax.fori_loop(0, CHUNKS + max(LAG_D + 1, LAG_E) + 2, step, 0)
 
     def sent(r, carry):
         pl.when(n_reg_next)(lambda: near(r).wait_send())
@@ -498,7 +499,7 @@
             pltpu.SemaphoreType.DMA((KINDS, CHUNKS)),
         ],
         compiler_params=pltpu.CompilerParams(
-            collective_id=0, has_side_effects=True, vmem_limit_bytes=55836672
+            collective_id=0, has_side_effects=True, vmem_limit_bytes=52 * 1024 * 1024
         ),
     )(
         images,

time: 89.7 us -> 85.6 us (0.954); the launches traced: 88.3 us -> 85.3 us
  Pallas kernels: 82.9 us -> 80 us
    pallas_call x1, Pallas kernels: 82.9 us -> 80 us  [on_device(): pl.pallas_call(kernel, out_shape=(jax.ShapeDtypeStruct((CAP, D), BF16), j...]
    unnamed x8 -> x10, local copies, waits for them, and re-layouts: 3.42 us -> 3.3 us
where the time goes in v2:
time: 85.6 us; the launch traced here: 85.3 us
  Pallas kernels  80 us (93%)
  local copies, waits for them, and re-layouts  3.3 us (4%)
  between operations  2 us (2%)
    pallas_call x1, Pallas kernels, on_device(): pl.pallas_call(kernel, out_shape=(jax.ShapeDtypeStruct((CAP, D), BF16), j...  80 us
    unnamed x10, local copies, waits for them, and re-layouts  3.3 us

profile of v2, /device:TPU:1, one launch (start us, length us, event | category | flops | bytes accessed | tf_op | source)
XLA Modules:
  0.0 85.3 jit_solution(14478510167473434556)
XLA Ops:
  0.6 0.0 copy-start.1
  1.3 0.0 copy-start.3
  2.0 0.0 copy-done.1
  2.0 0.0 copy-done.3
  2.0 0.0 copy-start
  2.0 1.0 %copy-done = bf16[192,1152]{1,0:T(8,128)(2,1)S(1)} copy-done((bf16[192,1152]{1,0:T(8,128)(2,1)S(1)}, bf16[192,1152]{1,0:T(8,128)(2,1)}, u32[]{:S(2)}) %copy-start) | copy-done | bytes 442392
  3.0 0.0 copy-start.2
  3.0 0.7 copy-done.2
  3.7 80.0 %shard_map.86 = (bf16[288,1152]{1,0:T(8,128)(2,1)S(1)}, bf16[192,1152]{1,0:T(8,128)(2,1)S(1)}) custom-call(bf16[192,1152]{1,0:T(8,128)(2,1)S(1)} %copy-done, bf16[288,1152]{1,0:T(8,128)(2,1)} %cap_hbm.1, s32[192]{0:T(256)S(1)} %copy-done.3, s32[288]{0:T(512)S(1)} %copy-done.1, s32[288]{0:T(512)S(1)} %copy-done.2, f32[1]{0:T(128)S(6)} %copy.11.gain_ref, ...), custom_call_target="tpu_custom_call" | custom-call | tf_op jit(solution)/shard_map/pallas_call | solution.py:455
  83.7 0.8 copy.13
  84.5 0.8 copy.14
Async XLA Ops:
  0.6 1.3 %copy-start.1 = (s32[288]{0:T(512)S(1)}, s32[288]{0:T(512)}, u32[]{:S(2)}) copy-start(s32[288]{0:T(512)} %own_hbm.1) | copy-start | bytes 3460
  1.3 0.7 copy-start.3
  2.0 1.0 %copy-start = (bf16[192,1152]{1,0:T(8,128)(2,1)S(1)}, bf16[192,1152]{1,0:T(8,128)(2,1)}, u32[]{:S(2)}) copy-start(bf16[192,1152]{1,0:T(8,128)(2,1)} %img_hbm.1) | copy-start | bytes 1327108
  3.0 0.7 copy-start.2

commit v3 on v2

--- a/solution.py
+++ b/solution.py
@@ -21,6 +21,7 @@
 LAG_D = 2
 LAG_Y = 4
 LAG_E = 5
+LAG_IN = 3
 
 NEAR, FAR, SIB1, SIB3, Q1, Q3, NEARB, FARB, EDGEN, EDGEF, RS1, RS2, EX, AG1, AG2, SWAP, SWAPB = range(17)
 FANN, FANF = 17, 20
@@ -56,6 +57,7 @@
     n_out_x, f_out_x = mm == HALF - 1, mm >= HALF - 2
     n_in_x, f_in_x = mm == 0, mm <= 1
     second = mm == 1
+    middle = jnp.logical_and(mm > 1, mm < HALF - 2)
     n_reg_next, f_reg_next = jnp.logical_not(n_out_x), jnp.logical_not(f_out_x)
     n_reg_prev, f_reg_prev = jnp.logical_not(n_in_x), jnp.logical_not(f_in_x)
     n_next = (lax.rem(blk + 2, BLKS), g)
@@ -395,15 +397,16 @@
         at(-3, stage_w)
         at(1, stage_c)
         at(0, stage_b)
-        at(LAG_D, stage_d)
+        at(LAG_D, stage_d, f_reg_prev)
+        at(LAG_IN, stage_d, f_in_x)
         at(LAG_Y, stage_y, f_out_x)
-        for k, stage in enumerate((stage_e, stage_f, stage_g)):
-            at(LAG_D + 1 + k, stage, f_reg_next)
-            at(LAG_E + k, stage, f_out_x)
+        for first, columns in ((LAG_D + 1, middle), (LAG_IN + 1, f_in_x), (LAG_E, f_out_x)):
+            for k, stage in enumerate((stage_e, stage_f, stage_g)):
+                at(first + k, stage, columns)
         pl.when(i == CHUNKS)(caption_out)
         return carry
 
-    lax.fori_loop(0, CHUNKS + max(LAG_D + 1, LAG_E) + 2, step, 0)
+    lax.fori_loop(0, CHUNKS + LAG_E + 2, step, 0)
 
     def sent(r, carry):
         pl.when(n_reg_next)(lambda: near(r).wait_send())

time: 85.6 us -> 85.5 us (level); the launches traced: 85.3 us -> 84.3 us
  Pallas kernels: 80 us -> 79 us
    pallas_call x1, Pallas kernels: 80 us -> 79 us  [on_device(): pl.pallas_call(kernel, out_shape=(jax.ShapeDtypeStruct((CAP, D), BF16), j...]
where the time goes in v3:
time: 85.5 us; the launch traced here: 84.3 us
  Pallas kernels  79 us (92%)
  local copies, waits for them, and re-layouts  3.3 us (4%)
  between operations  2 us (2%)
    pallas_call x1, Pallas kernels, on_device(): pl.pallas_call(kernel, out_shape=(jax.ShapeDtypeStruct((CAP, D), BF16), j...  79 us
    unnamed x10, local copies, waits for them, and re-layouts  3.3 us

profile of v3, /device:TPU:1, one launch (start us, length us, event | category | flops | bytes accessed | tf_op | source)
XLA Modules:
  0.0 84.3 jit_solution(2549339407688130835)
XLA Ops:
  0.6 0.0 copy-start.1
  1.3 0.0 copy-start.3
  2.0 0.0 copy-done.1
  2.0 0.0 copy-done.3
  2.0 0.0 copy-start
  2.0 1.0 %copy-done = bf16[192,1152]{1,0:T(8,128)(2,1)S(1)} copy-done((bf16[192,1152]{1,0:T(8,128)(2,1)S(1)}, bf16[192,1152]{1,0:T(8,128)(2,1)}, u32[]{:S(2)}) %copy-start) | copy-done | bytes 442392
  3.0 0.0 copy-start.2
  3.0 0.7 copy-done.2
  3.7 79.0 %shard_map.86 = (bf16[288,1152]{1,0:T(8,128)(2,1)S(1)}, bf16[192,1152]{1,0:T(8,128)(2,1)S(1)}) custom-call(bf16[192,1152]{1,0:T(8,128)(2,1)S(1)} %copy-done, bf16[288,1152]{1,0:T(8,128)(2,1)} %cap_hbm.1, s32[192]{0:T(256)S(1)} %copy-done.3, s32[288]{0:T(512)S(1)} %copy-done.1, s32[288]{0:T(512)S(1)} %copy-done.2, f32[1]{0:T(128)S(6)} %copy.11.gain_ref, ...), custom_call_target="tpu_custom_call" | custom-call | tf_op jit(solution)/shard_map/pallas_call | solution.py:458
  82.7 0.8 copy.13
  83.6 0.8 copy.14
Async XLA Ops:
  0.6 1.3 %copy-start.1 = (s32[288]{0:T(512)S(1)}, s32[288]{0:T(512)}, u32[]{:S(2)}) copy-start(s32[288]{0:T(512)} %own_hbm.1) | copy-start | bytes 3460
  1.3 0.7 copy-start.3
  2.0 1.0 %copy-start = (bf16[192,1152]{1,0:T(8,128)(2,1)S(1)}, bf16[192,1152]{1,0:T(8,128)(2,1)}, u32[]{:S(2)}) copy-start(bf16[192,1152]{1,0:T(8,128)(2,1)} %img_hbm.1) | copy-start | bytes 1327108
  3.0 0.7 copy-start.2
